TPU v7x, 32 devices: a whole 2x2x4 slice. The times are simulated.
32 devices in a mesh: groups: 2 (over x), face: 8 (over z, y), tile: 2 (over core).
Axes of the slice: x: 2, y: 2, z: 4, core: 2. Of those that a mesh axis runs over, the one named last changes fastest.
Arguments:
- fields: float32 [32, 64, 128, 128], P(('groups', 'face'), None, 'tile'), parts along dimension 0, may hold values from -8 to 8
- cotangent: float32 [32, 64, 128, 128], P(('groups', 'face'), None, 'tile'), parts along dimension 0, may hold values from -0.125 to 0.125
- first_kernel: float32 [64, 64, 3, 3], replicated, may hold values from -0.25 to 0.25
- second_kernel: float32 [64, 64, 3, 3], replicated, may hold values from -0.25 to 0.25
- coarse_kernel: float32 [64, 64, 3, 3], replicated, may hold values from -0.25 to 0.25
- slot_faces: int32 [16], replicated, may hold values from -1 to 11, as said below
- edge_table: int32 [16, 4, 2], replicated, may hold values from 0 to 15, as said below
- corner_table: int32 [16, 4, 3], replicated, may hold values from 0 to 15, as said below
Outputs:
- section_output: float32 [32, 64, 128, 128], P(('groups', 'face'), None, 'tile'), parts along dimension 0
- grad_first: float32 [128, 64, 3, 3], P('groups'), parts along dimension 0
- grad_second: float32 [128, 64, 3, 3], P('groups'), parts along dimension 0
- grad_coarse: float32 [128, 64, 3, 3], P('groups'), parts along dimension 0
There are 2 independent parts, one for each index of `groups`. A program takes and returns all parts, laid end to end along the dimension named above; an argument that names none is the same for every part. Nothing has to cross between parts.
Inputs may be any that keep to these rules, and one draw needn't show every extreme that they name: `slot_faces`: each face 0 to 11 stands in exactly one slot; the other slots hold -1. `edge_table`: for an occupied slot the entries follow the HEALPix base tessellation under the slot map; an empty slot names itself and its own side. The relation is symmetric: if side s of slot q names side t of slot p, then side t of p names side s of q. `corner_table`: entry [q, k, 2] is 1 where a fourth face meets diagonally at corner k, else 0 and the entry names slot q and corner k itself; empty slots name themselves. The relation is symmetric: if corner k of q names corner m of p, then corner m of p names corner k of q.
All inputs are finite; a program needn't handle non-finite values.
Results may differ from a plain program's by a relative error of at most 0.0003.
Values sent between devices are 32-bit elements; how exact they have to be, the bound alone decides.
A program may use at most 256 MiB of HBM per device.

v0:
```python
from functools import partial
import jax
import jax.numpy as jnp
from jax import lax
from jax.sharding import PartitionSpec as P

BLOCK = 4


def convolve(padded, kernel):
    return lax.conv_general_dilated(padded, kernel, (1, 1), "VALID", precision=lax.Precision.HIGH)


def activate(values):
    return jax.nn.gelu(values, approximate=False)


def activation_grad(values, grads):
    return jax.vjp(activate, lax.optimization_barrier(values))[1](grads)[0]


def split_sum(values, devices):
    turned = values.transpose(2, 3, 1, 0)
    shares = turned.reshape(devices, -1, 128)
    share = lax.psum_scatter(shares, ("face", "tile"), scatter_dimension=0, tiled=True)
    whole = lax.all_gather(share, ("face", "tile"), axis=0, tiled=True)
    return whole.reshape(turned.shape).transpose(3, 2, 0, 1)


def rim_pieces(tile_field):
    last_row = tile_field.shape[2] - 1
    last_col = tile_field.shape[3] - 1
    columns = jnp.stack([tile_field[:, :, :, 0], tile_field[:, :, :, last_col]], axis=1)[None]
    borders = jnp.stack([tile_field[:, :, 0, :], tile_field[:, :, last_row, :]], axis=1)[None]
    return (columns, borders)


def fine_gather(tile_field):
    columns, borders = rim_pieces(tile_field)
    tile_rows = columns.shape[-1]
    both = lax.all_gather(
        jnp.concatenate([columns, borders], axis=-1), ("face", "tile"), axis=0, tiled=True
    )
    return (both[..., :tile_rows], both[..., tile_rows:])


def fine_return(grad_columns, grad_borders):
    tile_rows = grad_columns.shape[-1]
    both = lax.psum_scatter(
        jnp.concatenate([grad_columns, grad_borders], axis=-1),
        ("face", "tile"),
        scatter_dimension=0,
        tiled=True,
    )
    return (both[..., :tile_rows], both[..., tile_rows:])


def fetch_lines(
    columns_all, borders_all, face_index, tile_index, face_count, tile_count, my_edges, my_corners
):
    slots_dev = columns_all.shape[1]
    channels = columns_all.shape[3]
    tile_rows = columns_all.shape[4]
    length = borders_all.shape[-1]
    cols_all = columns_all.reshape(face_count, tile_count, slots_dev, 2, channels, tile_rows)
    bord_all = borders_all.reshape(face_count, tile_count, slots_dev, 2, channels, length)
    near_slot = my_edges[:, :, 0]
    near_side = my_edges[:, :, 1]
    near_face = near_slot // slots_dev
    near_local = near_slot % slots_dev
    col_pick = jnp.where(near_side == 1, 1, 0)
    col_lines = cols_all[near_face, :, near_local, col_pick]
    col_lines = col_lines.transpose(0, 1, 3, 2, 4).reshape(
        slots_dev, 4, channels, tile_count * tile_rows
    )
    row_tile = jnp.where(near_side == 0, 0, tile_count - 1)
    row_pick = jnp.where(near_side == 0, 0, 1)
    row_lines = bord_all[near_face, row_tile, near_local, row_pick]
    halo_lines = jnp.where((near_side % 2 == 1)[:, :, None, None], col_lines, row_lines)
    corner_slot = my_corners[:, :, 0]
    corner_kind = my_corners[:, :, 1]
    corner_face = corner_slot // slots_dev
    corner_local = corner_slot % slots_dev
    corner_tile = jnp.where(corner_kind < 2, 0, tile_count - 1)
    corner_row = jnp.where(corner_kind < 2, 0, 1)
    corner_col = jnp.where((corner_kind == 0) | (corner_kind == 3), 0, length - 1)
    picked = bord_all[corner_face, corner_tile, corner_local, corner_row, :, corner_col]
    above_tile = bord_all[face_index, jnp.maximum(tile_index - 1, 0), :, 1]
    below_tile = bord_all[face_index, jnp.minimum(tile_index + 1, tile_count - 1), :, 0]
    return (halo_lines, picked, above_tile, below_tile)


def assemble(tile_field, pieces, tile_index, tile_count, my_corners):
    halo_lines, picked, above_tile, below_tile = pieces
    tile_rows = tile_field.shape[2]
    corner_flag = my_corners[:, :, 2]
    south_east = halo_lines[:, 0]
    north_east = halo_lines[:, 1]
    north_west = halo_lines[:, 2]
    south_west = halo_lines[:, 3]
    averaged = jnp.stack(
        [
            0.5 * (south_east[..., 0] + south_west[..., 0]),
            0.5 * (south_east[..., -1] + north_east[..., 0]),
            0.5 * (north_west[..., -1] + north_east[..., -1]),
            0.5 * (north_west[..., 0] + south_west[..., -1]),
        ],
        axis=1,
    )
    corners = jnp.where((corner_flag == 1)[:, :, None], picked, averaged)
    west_line = jnp.concatenate(
        [corners[:, 0, :, None], south_west, corners[:, 3, :, None]], axis=-1
    )
    east_line = jnp.concatenate(
        [corners[:, 1, :, None], north_east, corners[:, 2, :, None]], axis=-1
    )
    west_part = lax.dynamic_slice_in_dim(west_line, tile_index * tile_rows, tile_rows + 2, axis=2)
    east_part = lax.dynamic_slice_in_dim(east_line, tile_index * tile_rows, tile_rows + 2, axis=2)
    above_row = jnp.where(tile_index == 0, south_east, above_tile)
    below_row = jnp.where(tile_index == tile_count - 1, north_west, below_tile)
    top_row = jnp.concatenate([west_part[..., :1], above_row, east_part[..., :1]], axis=-1)
    bottom = jnp.concatenate([west_part[..., -1:], below_row, east_part[..., -1:]], axis=-1)
    middle = jnp.concatenate(
        [west_part[..., 1:-1, None], tile_field, east_part[..., 1:-1, None]], axis=-1
    )
    return jnp.concatenate([top_row[:, :, None], middle, bottom[:, :, None]], axis=2)


def framed_tile(
    tile_field,
    columns_all,
    borders_all,
    face_index,
    tile_index,
    face_count,
    tile_count,
    my_edges,
    my_corners,
):
    pieces = fetch_lines(
        columns_all,
        borders_all,
        face_index,
        tile_index,
        face_count,
        tile_count,
        my_edges,
        my_corners,
    )
    return assemble(tile_field, pieces, tile_index, tile_count, my_corners)


def local(
    fields,
    cotangent,
    first_kernel,
    second_kernel,
    coarse_kernel,
    slot_faces,
    edge_table,
    corner_table,
):
    face_index = lax.axis_index("face")
    tile_index = lax.axis_index("tile")
    face_count = lax.axis_size("face")
    tile_count = lax.axis_size("tile")
    slots_dev = fields.shape[0]
    my_slots = face_index * slots_dev + jnp.arange(slots_dev, dtype=jnp.int32)
    my_edges = edge_table[my_slots]
    my_corners = corner_table[my_slots]
    occupied = (slot_faces[my_slots] >= 0).astype(jnp.float32)[:, None, None, None]
    framer = partial(
        framed_tile,
        face_index=face_index,
        tile_index=tile_index,
        face_count=face_count,
        tile_count=tile_count,
        my_edges=my_edges,
        my_corners=my_corners,
    )
    columns_in, borders_in = fine_gather(fields)
    padded_in = framer(fields, columns_in, borders_in)
    first_act = convolve(padded_in, first_kernel)
    hidden = activate(first_act)
    columns_mid, borders_mid = fine_gather(hidden)
    padded_mid, frame_pull = jax.vjp(framer, hidden, columns_mid, borders_mid)
    second_act, second_pull = jax.vjp(convolve, padded_mid, second_kernel)
    features = activate(second_act)
    channels = features.shape[1]
    tile_rows = features.shape[2]
    length = features.shape[3]
    coarse = features.reshape(
        slots_dev, channels, tile_rows // BLOCK, BLOCK, length // BLOCK, BLOCK
    ).mean(axis=(3, 5))
    columns_low, borders_low = fine_gather(coarse)
    padded_low, low_pull = jax.vjp(framer, coarse, columns_low, borders_low)
    coarse_act, coarse_pull = jax.vjp(convolve, padded_low, coarse_kernel)
    bottleneck, bottleneck_pull = jax.vjp(activate, coarse_act)
    widened = jnp.repeat(jnp.repeat(bottleneck, BLOCK, axis=2), BLOCK, axis=3)
    section_output = (features + widened) * occupied
    masked = cotangent * occupied
    grad_bottleneck = masked.reshape(
        slots_dev, channels, tile_rows // BLOCK, BLOCK, length // BLOCK, BLOCK
    ).sum(axis=(3, 5))
    (grad_coarse_act,) = bottleneck_pull(grad_bottleneck)
    grad_padded_low, grad_coarse = coarse_pull(grad_coarse_act)
    grad_local, grad_columns_low, grad_borders_low = low_pull(grad_padded_low)
    back_low = fine_return(grad_columns_low, grad_borders_low)
    (spread_low,) = jax.vjp(rim_pieces, coarse)[1](back_low)
    grad_low = grad_local + spread_low
    grad_features = masked + jnp.repeat(jnp.repeat(grad_low, BLOCK, axis=2), BLOCK, axis=3) / (
        BLOCK * BLOCK
    )
    grad_second_act = activation_grad(second_act, grad_features)
    grad_padded_mid, grad_second = second_pull(grad_second_act)
    grad_hidden_local, grad_columns_mid, grad_borders_mid = frame_pull(grad_padded_mid)
    back_mid = fine_return(grad_columns_mid, grad_borders_mid)
    (spread_mid,) = jax.vjp(rim_pieces, hidden)[1](back_mid)
    grad_hidden = grad_hidden_local + spread_mid
    grad_second, grad_hidden = lax.optimization_barrier((grad_second, grad_hidden))
    grad_first_act = activation_grad(first_act, grad_hidden)
    (grad_first,) = jax.vjp(partial(convolve, padded_in), first_kernel)[1](grad_first_act)
    grad_second, grad_coarse = lax.psum((grad_second, grad_coarse), ("face", "tile"))
    grad_first = split_sum(grad_first, face_count * tile_count)
    return (section_output, grad_first, grad_second, grad_coarse)


def solution(mesh):
    in_specs = (
        P(("groups", "face"), None, "tile", None),
        P(("groups", "face"), None, "tile", None),
        P(),
        P(),
        P(),
        P(),
        P(),
        P(),
    )
    out_specs = (
        P(("groups", "face"), None, "tile", None),
        P("groups", None, None, None),
        P("groups", None, None, None),
        P("groups", None, None, None),
    )
    return jax.shard_map(local, mesh=mesh, in_specs=in_specs, out_specs=out_specs, check_vma=False)
```

profile of v0, /device:TPU:0, one launch (start us, length us, event | category | flops | bytes accessed | tf_op | source)
XLA Modules:
  0.0 1057.5 jit_solution(6484097872183846274)
XLA Ops:
  8.6 8.1 fusion.190
  23.6 8.4 copy.804
  34.7 42.5 %all-gather.3.cloned.1.call-done = f32[16,2,2,64,192]{4,3,2,1,0:T(8,128)} async-done(((f32[1,2,2,64,192]{4,3,2,1,0:T(8,128)}), f32[16,2,2,64,192]{4,3,2,1,0:T(8,128)}) %all-gather.3.cloned.1.call-update) | async-done | bytes 3145744 | tf_op jit(solution)/shard_map/all_gather | solution.py:41
  91.8 28.1 %fusion.217 = f32[64,66,2,130]{0,2,3,1:T(2,128)S(1)} fusion(f32[2,64,1,130]{1,0,3,2:T(2,128)S(1)} %maximum_bitcast_fusion.2, f32[2,64,64,1]{1,0,3,2:T(2,128)S(1)} %slice_bitcast_fusion.17, f32[2,64,64,128]{1,0,3,2:T(2,128)} %copy.804, f32[2,64,64,1]{1,0,3,2:T(2,128)S(1)} %slice_bitcast_fusion.18, f32[2,64,1,130]{1,0,3,2:T(2,128)S(1)} %maximum_bitcast_fusion.1), kind=kLoop, calls=%fused_computation.508 | loop fusion | flops 4392960 | bytes 8785920 | tf_op jit(solution)/shard_map/concatenate | solution.py:126
  124.5 72.1 %fusion.13 = (f32[64,16,17,64]{3,1,2,0:T(8,128)S(1)}, f32[64,16,17,64]{3,1,2,0:T(8,128)}) fusion(f32[64,64,3,3]{1,0,3,2:T(8,128)S(1)} %copy-done.51, f32[64,66,2,7,2]{0,3,2,4,1:T(8,128)S(1)} %slice.518, f32[64,66,2,8,17]{0,3,2,4,1:T(8,128)S(1)} %copy.808, pred[16,17]{0,1:T(8,128)(4,1)S(1)} %copy-done.55), kind=kOutput, calls=%fused_computation.36 | convolution fusion | flops 3926640640 | bytes 14129424 | tf_op jit(solution)/shard_map/conv_general_dilated | solution.py:11
  200.2 6.4 copy.809
  208.6 9.7 copy.1001
  226.7 6.6 copy.849
  237.5 9.0 copy.926
  246.5 25.5 %all-gather.5.cloned.1.call-done = f32[16,2,2,64,192]{4,3,2,1,0:T(8,128)} async-done(((f32[1,2,2,64,192]{4,3,2,1,0:T(8,128)}), f32[16,2,2,64,192]{4,3,2,1,0:T(8,128)}) %all-gather.5.cloned.1.call-update) | async-done | bytes 3145744 | tf_op jit(solution)/shard_map/all_gather | solution.py:41
  285.8 28.1 %fusion.216 = f32[64,66,2,130]{0,2,3,1:T(2,128)S(1)} fusion(f32[2,64,1,130]{1,0,3,2:T(2,128)S(1)} %maximum_bitcast_fusion.4, f32[2,64,64,1]{1,0,3,2:T(2,128)S(1)} %slice_bitcast_fusion.13, f32[2,64,64,128]{1,0,3,2:T(2,128)} %bitcast.462, f32[2,64,64,1]{1,0,3,2:T(2,128)S(1)} %slice_bitcast_fusion.14, f32[2,64,1,130]{1,0,3,2:T(2,128)S(1)} %maximum_bitcast_fusion.3), kind=kLoop, calls=%fused_computation.507 | loop fusion | flops 4392960 | bytes 8785920 | tf_op jit(solution)/shard_map/jvp()/concatenate | solution.py:126
  318.4 63.1 %fusion.15 = (f32[64,16,17,64]{3,1,2,0:T(8,128)S(1)}, f32[64,16,17,64]{3,1,2,0:T(8,128)}) fusion(f32[64,64,3,3]{1,0,3,2:T(8,128)S(1)} %copy-done, f32[64,66,2,7,2]{0,3,2,4,1:T(8,128)S(1)} %slice.550, f32[64,66,2,8,17]{0,3,2,4,1:T(8,128)S(1)} %copy.827, pred[16,17]{0,1:T(8,128)(4,1)S(1)} %copy-done.55), kind=kOutput, calls=%fused_computation.38 | convolution fusion | flops 3926640640 | bytes 14129424 | tf_op jit(solution)/shard_map/jvp()/conv_general_dilated | solution.py:11
  381.5 6.2 copy.828
  387.7 12.2 %fusion.188 = (f32[64,2,128,64]{3,0,2,1:T(8,128)}, f32[2,64,64,128]{1,2,3,0:T(8,128)}) fusion(f32[64,2,136,64]{3,0,2,1:T(8,128)} %bitcast.464), kind=kLoop, calls=%fused_computation.488 | loop fusion | bytes 12582912 | tf_op jit(solution)/shard_map/mul | solution.py:15
  399.9 11.6 %copy.830 = f32[2,64,64,128]{1,3,2,0:T(8,128)} copy(f32[2,64,64,128]{1,2,3,0:T(8,128)} %get-tuple-element.63) | data formatting | bytes 8388608 | tf_op jit(solution)/shard_map/mul | solution.py:15
  411.4 6.5 reduce_sum.58
  418.6 25.3 %all_gather.14 = f32[16,2,2,64,48]{3,4,2,1,0:T(8,128)S(1)} all-gather(f32[1,2,2,64,48]{3,4,2,1,0:T(8,128)S(1)} %pad_maximum_fusion.7), channel_id=1, replica_groups=mesh['groups'=2,'face'=8,'tile'=2] {'face','tile'}, dimensions={0}, use_global_device_ids=true | all-gather | bytes 835584 | tf_op jit(solution)/shard_map/all_gather | solution.py:41
  448.4 5.0 broadcast_multiply_fusion.1
  462.2 8.0 copy.848
  470.3 8.8 copy.925
  479.1 10.5 broadcast_multiply_fusion
  489.6 7.2 copy.855
  498.2 6.1 reduce_sum.62
  513.9 6.5 copy.851
  524.6 9.3 copy.927
  534.0 5.0 fusion.76
  538.9 32.1 %reduce-scatter.6.cloned.1.call-done = f32[1,2,2,64,48]{3,4,2,1,0:T(8,128)} async-done(((f32[16,2,2,64,48]{3,4,2,1,0:T(8,128)}), f32[1,2,2,64,48]{3,4,2,1,0:T(8,128)}) %reduce-scatter.6.cloned.1.call-update) | async-done | bytes 49168 | tf_op jit(solution)/shard_map/reduce_scatter | solution.py:49
  581.7 8.1 copy.880
  589.8 12.6 %fusion.39 = f32[2,64,64,128]{3,2,1,0:T(8,128)} fusion(f32[2,64,64,128]{3,2,1,0:T(8,128)} %get-tuple-element.193, f32[2,64,64,128]{3,2,1,0:T(8,128)} %copy.880, f32[2,64,64,128]{3,2,1,0:T(8,128)} %bitcast.474), kind=kLoop, calls=%fused_computation.84 | loop fusion | flops 75497472 | bytes 16777216 | tf_op jit(solution)/shard_map/transpose(jvp())/add_any | solution.py:15
  602.4 8.4 copy.881
  610.8 9.3 copy.941
  628.0 9.7 select_maximum_fusion.2
  637.7 11.3 %copy.883 = f32[64,64,2,8,19]{0,3,2,4,1:T(8,128)} copy(f32[64,64,2,8,19]{1,0,4,3,2:T(8,128)} %select_maximum_fusion.2) | data formatting | bytes 9961472 | tf_op jit(solution)/shard_map/transpose(jvp())/conv_general_dilated | solution.py:11
  649.0 25.5 %broadcast_select_fusion = f32[66,16,17,64]{3,1,2,0:T(8,128)} fusion(pred[16,17]{0,1:T(8,128)(4,1)S(1)} %copy-done.54, f32[64,64,3,3]{1,0,3,2:T(8,128)S(1)} %copy-done, f32[64,64,2,8,19]{0,3,2,4,1:T(8,128)} %copy.883), kind=kOutput, calls=%fused_computation.78 | convolution fusion | flops 3851520000 | bytes 9724176 | tf_op jit(solution)/shard_map/transpose(jvp())/conv_general_dilated | solution.py:11
  674.4 11.3 %copy.884 = f32[66,16,17,64]{0,3,2,1:T(8,128)} copy(f32[66,16,17,64]{3,1,2,0:T(8,128)} %broadcast_select_fusion) | data formatting | bytes 9191424 | tf_op jit(solution)/shard_map/transpose(jvp())/conv_general_dilated | solution.py:11
  686.7 8.6 slice.597
  695.3 11.4 %copy.935 = f32[66,2,130,64]{2,0,3,1:T(8,128)} copy(f32[66,2,130,64]{0,3,2,1:T(8,128)} %slice.597) | data formatting | bytes 8785920
  713.6 5.2 copy.894
  718.8 8.4 fusion.186
  727.2 4.9 copy.914
  732.3 4.9 copy.915
  755.4 93.1 %fusion.204 = f32[64,64,3,3]{0,1,3,2:T(8,128)} fusion(f32[2,64,64,128]{1,0,3,2:T(2,128)} %copy.881, f32[2,64,1,130]{1,0,3,2:T(2,128)S(1)} %copy-done.17, f32[2,64,64,1]{1,0,3,2:T(2,128)S(1)} %copy-done.27, f32[2,64,64,128]{1,0,3,2:T(2,128)} %bitcast.463, f32[2,64,64,1]{1,0,3,2:T(2,128)S(1)} %copy-done.29, f32[2,64,1,130]{1,0,3,2:T(2,128)S(1)} %copy-done.19), kind=kOutput, calls=%fused_computation.504 | convolution fusion | flops 3628271616 | bytes 8734720 | tf_op jit(solution)/shard_map/transpose(jvp())/conv_general_dilated | solution.py:11
  855.2 7.5 slice_add_fusion
  862.7 10.7 %fusion.43 = f32[2,64,64,128]{3,2,1,0:T(8,128)} fusion(f32[2,64,64,128]{3,2,1,0:T(8,128)S(1)} %slice_add_fusion, f32[2,64,64,128]{3,2,1,0:T(8,128)S(1)} %bitcast.473), kind=kLoop, calls=%fused_computation.88 | loop fusion | flops 74448896 | bytes 12582912 | tf_op jit(solution)/shard_map/transpose(jvp())/add_any | solution.py:15
  873.4 8.5 copy.903
  882.1 91.9 %fusion.205 = f32[3,3,64,64]{3,2,1,0:T(8,128)S(1)} fusion(f32[2,64,64,128]{1,0,3,2:T(2,128)} %copy.903, f32[2,64,1,130]{1,0,3,2:T(2,128)S(1)} %copy-done.13, f32[2,64,64,1]{1,0,3,2:T(2,128)S(1)} %copy-done.23, f32[2,64,64,128]{1,0,3,2:T(2,128)} %copy.804, f32[2,64,64,1]{1,0,3,2:T(2,128)S(1)} %copy-done.25, f32[2,64,1,130]{1,0,3,2:T(2,128)S(1)} %copy-done.15), kind=kOutput, calls=%fused_computation.505 | convolution fusion | flops 3628271616 | bytes 8734720 | tf_op jit(solution)/shard_map/transpose | solution.py:23
  978.5 50.8 %reduce-scatter.10.cloned.1.call-done = f32[1,18,128]{2,1,0:T(8,128)} async-done(((f32[16,18,128]{2,1,0:T(8,128)}), f32[1,18,128]{2,1,0:T(8,128)}) %reduce-scatter.10.cloned.1.call-update) | async-done | bytes 9232
  1029.3 20.2 %all_gather.15 = f32[16,18,128]{2,1,0:T(8,128)S(1)} all-gather(f32[1,18,128]{2,1,0:T(8,128)} %reduce-scatter.10.cloned.1.call-done), channel_id=1, replica_groups=mesh['groups'=2,'face'=8,'tile'=2] {'face','tile'}, dimensions={0}, use_global_device_ids=true | all-gather | bytes 156672 | tf_op jit(solution)/shard_map/all_gather | solution.py:26
  (372 shorter events, 151.1 us)
Async XLA Ops:
  7.2 311.2 %copy-start = (f32[64,64,3,3]{1,0,3,2:T(8,128)S(1)}, f32[64,64,3,3]{1,0,3,2:T(8,128)}, u32[]{:S(2)}) copy-start(f32[64,64,3,3]{1,0,3,2:T(8,128)} %param.11) | copy-start | bytes 442372
  7.2 70.0 %all-gather.3.cloned.1.call-start = ((), (), s32[]{:S(2)}) async-start(), calls=%async_computation.3 | async-start | bytes 4456448 | tf_op jit(solution)/shard_map/all_gather | solution.py:41
  23.6 248.4 %all-gather.5.cloned.1.call-start = ((), (), s32[]{:S(2)}) async-start(), calls=%async_computation.4 | async-start | bytes 4456448 | tf_op jit(solution)/shard_map/all_gather | solution.py:41
  23.6 8.4 copy-start.46
  23.6 8.5 copy-start.47
  34.7 411.5 %copy-start.43 = (pred[2,4,1]{0,1,2:T(4,128)(4,1)}, pred[2,4,1]{0,1,2:T(4,128)(4,1)S(1)}, u32[]{:S(2)}) copy-start(pred[2,4,1]{0,1,2:T(4,128)(4,1)S(1)} %copy.909) | copy-start | bytes 28
  90.2 29.8 %copy-start.22 = (f32[2,64,64,1]{1,0,3,2:T(2,128)}, f32[2,64,64,1]{1,0,3,2:T(2,128)S(1)}, u32[]{:S(2)}) copy-start(f32[2,64,64,1]{1,0,3,2:T(2,128)S(1)} %slice_bitcast_fusion.17) | copy-start | bytes 98308
  90.3 29.7 %copy-start.24 = (f32[2,64,64,1]{1,0,3,2:T(2,128)}, f32[2,64,64,1]{1,0,3,2:T(2,128)S(1)}, u32[]{:S(2)}) copy-start(f32[2,64,64,1]{1,0,3,2:T(2,128)S(1)} %slice_bitcast_fusion.18) | copy-start | bytes 98308
  91.7 28.3 %copy-start.12 = (f32[2,64,1,130]{1,0,3,2:T(2,128)}, f32[2,64,1,130]{1,0,3,2:T(2,128)S(1)}, u32[]{:S(2)}) copy-start(f32[2,64,1,130]{1,0,3,2:T(2,128)S(1)} %maximum_bitcast_fusion.2) | copy-start | bytes 199684
  91.8 28.2 %copy-start.14 = (f32[2,64,1,130]{1,0,3,2:T(2,128)}, f32[2,64,1,130]{1,0,3,2:T(2,128)S(1)}, u32[]{:S(2)}) copy-start(f32[2,64,1,130]{1,0,3,2:T(2,128)S(1)} %maximum_bitcast_fusion.1) | copy-start | bytes 199684
  196.7 3.5 copy-start.6
  208.6 14.3 %copy-start.2 = (s32[16]{0:T(128)S(1)}, s32[16]{0:T(128)}, u32[]{:S(2)}) copy-start(s32[16]{0:T(128)} %param.13) | copy-start | bytes 196
  218.3 3.3 copy-start.4
  222.8 348.3 %reduce-scatter.6.cloned.1.call-start = ((), (), s32[]{:S(2)}) async-start(), calls=%async_computation.5 | async-start | bytes 1671168 | tf_op jit(solution)/shard_map/reduce_scatter | solution.py:49
  277.6 5.9 slice-start.1
  285.2 28.8 %copy-start.26 = (f32[2,64,64,1]{1,0,3,2:T(2,128)}, f32[2,64,64,1]{1,0,3,2:T(2,128)S(1)}, u32[]{:S(2)}) copy-start(f32[2,64,64,1]{1,0,3,2:T(2,128)S(1)} %slice_bitcast_fusion.13) | copy-start | bytes 98308
  285.3 28.7 %copy-start.28 = (f32[2,64,64,1]{1,0,3,2:T(2,128)}, f32[2,64,64,1]{1,0,3,2:T(2,128)S(1)}, u32[]{:S(2)}) copy-start(f32[2,64,64,1]{1,0,3,2:T(2,128)S(1)} %slice_bitcast_fusion.14) | copy-start | bytes 98308
  285.7 28.3 %copy-start.16 = (f32[2,64,1,130]{1,0,3,2:T(2,128)}, f32[2,64,1,130]{1,0,3,2:T(2,128)S(1)}, u32[]{:S(2)}) copy-start(f32[2,64,1,130]{1,0,3,2:T(2,128)S(1)} %maximum_bitcast_fusion.4) | copy-start | bytes 199684
  285.8 28.2 %copy-start.18 = (f32[2,64,1,130]{1,0,3,2:T(2,128)}, f32[2,64,1,130]{1,0,3,2:T(2,128)S(1)}, u32[]{:S(2)}) copy-start(f32[2,64,1,130]{1,0,3,2:T(2,128)S(1)} %maximum_bitcast_fusion.3) | copy-start | bytes 199684
  444.0 4.4 copy-start.52
  444.0 4.4 copy-start.57
  446.3 7.2 copy-start.37
  446.4 7.1 copy-start.39
  470.3 8.8 copy-start.50
  489.6 7.3 copy-start.11
  489.6 7.5 copy-start.10
  507.6 2.9 copy-start.42
  507.7 3.9 copy-start.35
  513.9 334.6 %reduce-scatter.8.cloned.1.call-start = ((), (), s32[]{:S(2)}) async-start(), calls=%async_computation.6 | async-start | bytes 4456448 | tf_op jit(solution)/shard_map/reduce_scatter | solution.py:49
  524.6 9.3 copy-start.8
  524.6 9.3 copy-start.32
  524.6 9.3 copy-start.34
  524.6 9.3 copy-start.38
  524.6 9.3 copy-start.40
  624.5 3.4 copy-start.3
  637.7 11.3 %copy-start.54 = (pred[16,17]{0,1:T(8,128)(4,1)S(1)}, pred[16,17]{0,1:T(8,128)(4,1)}, u32[]{:S(2)}) copy-start(pred[16,17]{0,1:T(8,128)(4,1)} %constant.351) | copy-start | bytes 820
  727.2 4.9 copy-start.48
  727.2 10.1 copy-start.45
  738.0 4.1 copy-start.41
  754.4 220.4 %all-reduce.50.cloned.1.call-start = ((), (), s32[]{:S(2)}) async-start(), calls=%async_computation.8 | async-start | bytes 1179648 | tf_op jit(solution)/shard_map/psum | solution.py:223
  849.4 5.7 copy-start.30
  855.2 7.5 copy-start.5
  873.4 8.6 copy-start.13
  873.4 8.6 copy-start.15
  873.4 8.6 copy-start.23
  873.4 8.6 copy-start.25
  882.0 147.4 %reduce-scatter.10.cloned.1.call-start = ((), (), s32[]{:S(2)}) async-start(), calls=%async_computation.7 | async-start | bytes 208896
  882.1 168.4 %copy-start.1 = (f32[64,64,3,3]{1,0,3,2:T(8,128)S(1)}, f32[64,64,3,3]{1,0,3,2:T(8,128)}, u32[]{:S(2)}) copy-start(f32[64,64,3,3]{1,0,3,2:T(8,128)} %param.11) | copy-start | bytes 442372
  (18 other events, 22.3 us)
Sparse Core Ops, SparseCore 0:
  23.7 53.4 all-gather.2
  222.9 49.0 all-gather.4
  514.0 56.9 reduce-scatter.5
  754.5 71.3 reduce-scatter.7
  882.1 90.6 all-reduce.49
  976.7 52.5 reduce-scatter.9
where the time goes:
time: 1070 us; the launch traced here: 1060 us
  matrix products  358 us (33%)
  local copies, waits for them, and re-layouts  343 us (32%)
  waiting for transfers between devices  151 us (14%)
  other arithmetic  144 us (13%)
  blocking collectives  45.5 us (4%)
  between operations  16.2 us (2%)
    conv_general_dilated x7, matrix products, convolve(): lax.conv_general_dilated(padded, kernel, (1, 1), 'VALID', precision=lax.P...  266 us
    transpose x1, matrix products, split_sum(): turned = values.transpose(2, 3, 1, 0)  91.9 us
    unnamed x139, local copies, waits for them, and re-layouts  90.9 us
    all_gather x2, waiting for transfers between devices, fine_gather(): lax.all_gather(jnp.concatenate([columns, borders], axis=-1), ('face', 'ti...  68 us
    concatenate x3, other arithmetic, assemble(): jnp.concatenate([top_row[:, :, None], middle, bottom[:, :, None]], axis=2)  56.6 us
    conv_general_dilated x27, local copies, waits for them, and re-layouts, convolve(): lax.conv_general_dilated(padded, kernel, (1, 1), 'VALID', precision=lax.P...  56 us
    unnamed x7, waiting for transfers between devices  50.9 us
    mul x14, local copies, waits for them, and re-layouts, activate(): return jax.nn.gelu(values, approximate=False)  39 us
  transfers between devices with their start and end apart: 6, of which 4 were waited for; matrix products, arithmetic and copies ran while one was open for 24% of the time, Pallas kernels for 0%

commit v1 on v0

--- a/solution.py
+++ b/solution.py
@@ -38,9 +38,28 @@
 def fine_gather(tile_field):
     columns, borders = rim_pieces(tile_field)
     tile_rows = columns.shape[-1]
-    both = lax.all_gather(
-        jnp.concatenate([columns, borders], axis=-1), ("face", "tile"), axis=0, tiled=True
-    )
+    x = jnp.concatenate([columns, borders], axis=-1)
+    ways, here, lap = (
+        lax.axis_size(("face", "tile")),
+        lax.axis_index(("face", "tile")),
+        x.shape[0],
+    )
+    lengths = [n * ways if d == 0 else n for d, n in enumerate(x.shape)]
+    full = lax.dynamic_update_slice_in_dim(jnp.zeros(lengths, x.dtype), x, here * lap, axis=0)
+    going_up = going_down = x
+    for far in range(1, ways // 2 + 1):
+        going_up = lax.ppermute(
+            going_up, ("face", "tile"), [(d, (d + 1) % ways) for d in range(ways)]
+        )
+        full = lax.dynamic_update_slice_in_dim(full, going_up, (here - far) % ways * lap, axis=0)
+        if 2 * far < ways:
+            going_down = lax.ppermute(
+                going_down, ("face", "tile"), [(d, (d - 1) % ways) for d in range(ways)]
+            )
+            full = lax.dynamic_update_slice_in_dim(
+                full, going_down, (here + far) % ways * lap, axis=0
+            )
+    both = full
     return (both[..., :tile_rows], both[..., tile_rows:])
 
 

time: 1070 us -> 1200 us (1.12)
  starting transfers between devices: 0.25 us -> 99.6 us
  waiting for transfers between devices: 151 us -> 186 us
  blocking collectives: 45.5 us -> 20.2 us
  local copies, waits for them, and re-layouts: 343 us -> 366 us
    ppermute x0 -> x45, starting transfers between devices: none -> 99 us  [the longest x21 95.8 us: fine_gather(): lax.ppermute(going_down, ('face', 'tile'), [(d, (d - 1) % ways) for d in...]
    ppermute x0 -> x45, waiting for transfers between devices: none -> 84.4 us  [the longest x24 81.3 us: fine_gather(): lax.ppermute(going_up, ('face', 'tile'), [(d, (d + 1) % ways) for d in ra...]
    all_gather x2 -> x0, waiting for transfers between devices: 68 us -> none  [fine_gather(): lax.all_gather(jnp.concatenate([columns, borders], axis=-1), ('face', 'ti...]
    all_gather x1 -> x0, blocking collectives: 25.3 us -> none  [fine_gather(): lax.all_gather(jnp.concatenate([columns, borders], axis=-1), ('face', 'ti...]
    reduce_scatter x2, waiting for transfers between devices: 32.1 us -> 50.6 us  [fine_return(): lax.psum_scatter(jnp.concatenate([grad_columns, grad_borders], axis=-1),...]
    dynamic_update_slice x0 -> x46, local copies, waits for them, and re-layouts: none -> 13.2 us  [the longest x24 6.68 us: fine_gather(): lax.dynamic_update_slice_in_dim(full, going_up, (here - far) % ways * lap...]
    unnamed x139 -> x143, local copies, waits for them, and re-layouts: 90.9 us -> 88.7 us
    unnamed x7 -> x5, waiting for transfers between devices: 50.9 us -> 50.7 us
  transfers between devices with their start and end apart: 6 -> 49, of which waited for: 4 -> 30; matrix products, arithmetic and copies ran while one was open for 24% -> 23% of each run, Pallas kernels for 0% -> 0%
where the time goes in v1:
time: 1200 us; the launch traced here: 1190 us
  local copies, waits for them, and re-layouts  366 us (30%)
  matrix products  359 us (30%)
  waiting for transfers between devices  186 us (16%)
  other arithmetic  144 us (12%)
  starting transfers between devices  99.6 us (8%)
  blocking collectives  20.2 us (2%)
  between operations  16.8 us (1%)
    conv_general_dilated x7, matrix products, convolve(): lax.conv_general_dilated(padded, kernel, (1, 1), 'VALID', precision=lax.P...  267 us
    ppermute x21, starting transfers between devices, fine_gather(): lax.ppermute(going_down, ('face', 'tile'), [(d, (d - 1) % ways) for d in...  95.8 us
    transpose x1, matrix products, split_sum(): turned = values.transpose(2, 3, 1, 0)  92.1 us
    unnamed x143, local copies, waits for them, and re-layouts  88.7 us
    ppermute x24, waiting for transfers between devices, fine_gather(): lax.ppermute(going_up, ('face', 'tile'), [(d, (d + 1) % ways) for d in ra...  81.3 us
    concatenate x3, other arithmetic, assemble(): jnp.concatenate([top_row[:, :, None], middle, bottom[:, :, None]], axis=2)  56.6 us
    conv_general_dilated x27, local copies, waits for them, and re-layouts, convolve(): lax.conv_general_dilated(padded, kernel, (1, 1), 'VALID', precision=lax.P...  55.7 us
    unnamed x5, waiting for transfers between devices  50.7 us
  transfers between devices with their start and end apart: 49, of which 30 were waited for; matrix products, arithmetic and copies ran while one was open for 23% of the time, Pallas kernels for 0%

profile of v1, /device:TPU:0, one launch (start us, length us, event | category | flops | bytes accessed | tf_op | source)
XLA Modules:
  0.0 1190.6 jit_solution(5439815567765777399)
XLA Ops:
  8.6 8.1 fusion.189
  23.3 5.1 collective-permute-start.1
  28.9 8.4 copy.1108
  100.5 6.7 collective-permute-done.14
  125.4 28.1 %fusion.216 = f32[64,66,2,130]{0,2,3,1:T(2,128)S(1)} fusion(f32[2,64,1,130]{1,0,3,2:T(2,128)S(1)} %maximum_bitcast_fusion.2, f32[2,64,64,1]{1,0,3,2:T(2,128)S(1)} %slice_bitcast_fusion.17, f32[2,64,64,128]{1,0,3,2:T(2,128)} %copy.1108, f32[2,64,64,1]{1,0,3,2:T(2,128)S(1)} %slice_bitcast_fusion.18, f32[2,64,1,130]{1,0,3,2:T(2,128)S(1)} %maximum_bitcast_fusion.1), kind=kLoop, calls=%fused_computation.556 | loop fusion | flops 4392960 | bytes 8785920 | tf_op jit(solution)/shard_map/concatenate | solution.py:145
  158.2 72.1 %fusion.13 = (f32[64,16,17,64]{3,1,2,0:T(8,128)S(1)}, f32[64,16,17,64]{3,1,2,0:T(8,128)}) fusion(f32[64,64,3,3]{1,0,3,2:T(8,128)S(1)} %copy-done.53, f32[64,66,2,7,2]{0,3,2,4,1:T(8,128)S(1)} %slice.518, f32[64,66,2,8,17]{0,3,2,4,1:T(8,128)S(1)} %copy.1112, pred[16,17]{0,1:T(8,128)(4,1)S(1)} %copy-done.57), kind=kOutput, calls=%fused_computation.36 | convolution fusion | flops 3926640640 | bytes 14129424 | tf_op jit(solution)/shard_map/conv_general_dilated | solution.py:11
  233.8 6.4 copy.1113
  242.2 9.7 copy.1335
  325.8 9.3 collective-permute-done.29
  348.7 28.1 %fusion.215 = f32[64,66,2,130]{0,2,3,1:T(2,128)S(1)} fusion(f32[2,64,1,130]{1,0,3,2:T(2,128)S(1)} %maximum_bitcast_fusion.4, f32[2,64,64,1]{1,0,3,2:T(2,128)S(1)} %slice_bitcast_fusion.13, f32[2,64,64,128]{1,0,3,2:T(2,128)} %bitcast.460, f32[2,64,64,1]{1,0,3,2:T(2,128)S(1)} %slice_bitcast_fusion.14, f32[2,64,1,130]{1,0,3,2:T(2,128)S(1)} %maximum_bitcast_fusion.3), kind=kLoop, calls=%fused_computation.555 | loop fusion | flops 4392960 | bytes 8785920 | tf_op jit(solution)/shard_map/jvp()/concatenate | solution.py:145
  381.3 63.0 %fusion.15 = (f32[64,16,17,64]{3,1,2,0:T(8,128)S(1)}, f32[64,16,17,64]{3,1,2,0:T(8,128)}) fusion(f32[64,64,3,3]{1,0,3,2:T(8,128)S(1)} %copy-done, f32[64,66,2,7,2]{0,3,2,4,1:T(8,128)S(1)} %slice.550, f32[64,66,2,8,17]{0,3,2,4,1:T(8,128)S(1)} %copy.1146, pred[16,17]{0,1:T(8,128)(4,1)S(1)} %copy-done.57), kind=kOutput, calls=%fused_computation.38 | convolution fusion | flops 3926640640 | bytes 14129424 | tf_op jit(solution)/shard_map/jvp()/conv_general_dilated | solution.py:11
  444.3 6.3 copy.1147
  450.6 12.2 %fusion.187 = (f32[64,2,128,64]{3,0,2,1:T(8,128)}, f32[2,64,64,128]{1,2,3,0:T(8,128)}) fusion(f32[64,2,136,64]{3,0,2,1:T(8,128)} %bitcast.462), kind=kLoop, calls=%fused_computation.536 | loop fusion | bytes 12582912 | tf_op jit(solution)/shard_map/mul | solution.py:15
  462.8 11.6 copy.1149
  474.5 6.4 reduce_sum.58
  482.8 6.4 copy.1168
  493.4 8.8 copy.1244
  506.6 9.2 copy.1243
  515.8 6.4 copy.1170
  526.4 8.8 copy.1245
  576.3 6.7 collective-permute-done.44
  591.2 5.0 broadcast_multiply_fusion.1
  605.0 8.0 copy.1167
  613.0 10.5 broadcast_multiply_fusion
  623.6 7.3 copy.1174
  632.8 6.1 reduce_sum.62
  648.9 6.1 fusion.76
  655.0 50.6 %reduce-scatter.6.cloned.1.call-done = f32[1,2,2,64,48]{3,4,2,1,0:T(8,128)} async-done(((f32[16,2,2,64,48]{3,4,2,1,0:T(8,128)}), f32[1,2,2,64,48]{3,4,2,1,0:T(8,128)}) %reduce-scatter.6.cloned.1.call-update) | async-done | bytes 49168 | tf_op jit(solution)/shard_map/reduce_scatter | solution.py:68
  716.3 8.0 copy.1199
  724.3 12.7 %fusion.39 = f32[2,64,64,128]{3,2,1,0:T(8,128)} fusion(f32[2,64,64,128]{3,2,1,0:T(8,128)} %get-tuple-element.195, f32[2,64,64,128]{3,2,1,0:T(8,128)} %copy.1199, f32[2,64,64,128]{3,2,1,0:T(8,128)} %bitcast.472), kind=kLoop, calls=%fused_computation.84 | loop fusion | flops 75497472 | bytes 16777216 | tf_op jit(solution)/shard_map/transpose(jvp())/add_any | solution.py:15
  737.0 8.4 copy.1200
  745.4 9.2 copy.1259
  762.4 9.6 select_maximum_fusion.2
  772.1 11.3 copy.1202
  783.3 25.7 %broadcast_select_fusion = f32[66,16,17,64]{3,1,2,0:T(8,128)} fusion(pred[16,17]{0,1:T(8,128)(4,1)S(1)} %copy-done.56, f32[64,64,3,3]{1,0,3,2:T(8,128)S(1)} %copy-done, f32[64,64,2,8,19]{0,3,2,4,1:T(8,128)} %copy.1202), kind=kOutput, calls=%fused_computation.78 | convolution fusion | flops 3851520000 | bytes 9724176 | tf_op jit(solution)/shard_map/transpose(jvp())/conv_general_dilated | solution.py:11
  809.0 11.3 copy.1203
  821.3 8.5 slice.597
  829.8 11.2 copy.1253
  847.9 5.2 copy.1213
  853.1 8.4 fusion.185
  861.5 5.2 copy.1233
  889.2 92.9 %fusion.203 = f32[64,64,3,3]{0,1,3,2:T(8,128)} fusion(f32[2,64,64,128]{1,0,3,2:T(2,128)} %copy.1200, f32[2,64,1,130]{1,0,3,2:T(2,128)S(1)} %copy-done.15, f32[2,64,64,1]{1,0,3,2:T(2,128)S(1)} %copy-done.27, f32[2,64,64,128]{1,0,3,2:T(2,128)} %bitcast.461, f32[2,64,64,1]{1,0,3,2:T(2,128)S(1)} %copy-done.29, f32[2,64,1,130]{1,0,3,2:T(2,128)S(1)} %copy-done.17), kind=kOutput, calls=%fused_computation.552 | convolution fusion | flops 3628271616 | bytes 8734720 | tf_op jit(solution)/shard_map/transpose(jvp())/conv_general_dilated | solution.py:11
  988.6 7.5 slice_add_fusion
  996.1 10.7 fusion.43
  1006.8 8.4 copy.1222
  1015.3 92.1 %fusion.204 = f32[3,3,64,64]{3,2,1,0:T(8,128)S(1)} fusion(f32[2,64,64,128]{1,0,3,2:T(2,128)} %copy.1222, f32[2,64,1,130]{1,0,3,2:T(2,128)S(1)} %copy-done.11, f32[2,64,64,1]{1,0,3,2:T(2,128)S(1)} %copy-done.23, f32[2,64,64,128]{1,0,3,2:T(2,128)} %copy.1108, f32[2,64,64,1]{1,0,3,2:T(2,128)S(1)} %copy-done.25, f32[2,64,1,130]{1,0,3,2:T(2,128)S(1)} %copy-done.13), kind=kOutput, calls=%fused_computation.553 | convolution fusion | flops 3628271616 | bytes 8734720 | tf_op jit(solution)/shard_map/transpose | solution.py:23
  1111.9 50.6 %reduce-scatter.10.cloned.1.call-done = f32[1,18,128]{2,1,0:T(8,128)} async-done(((f32[16,18,128]{2,1,0:T(8,128)}), f32[1,18,128]{2,1,0:T(8,128)}) %reduce-scatter.10.cloned.1.call-update) | async-done | bytes 9232
  1162.5 20.2 %all_gather.3 = f32[16,18,128]{2,1,0:T(8,128)S(1)} all-gather(f32[1,18,128]{2,1,0:T(8,128)} %reduce-scatter.10.cloned.1.call-done), channel_id=1, replica_groups=mesh['groups'=2,'face'=8,'tile'=2] {'face','tile'}, dimensions={0}, use_global_device_ids=true | all-gather | bytes 156672 | tf_op jit(solution)/shard_map/all_gather | solution.py:26
  (522 shorter events, 335.1 us)
Async XLA Ops:
  7.2 698.4 %reduce-scatter.6.cloned.1.call-start = ((), (), s32[]{:S(2)}) async-start(), calls=%async_computation.3 | async-start | bytes 1671168 | tf_op jit(solution)/shard_map/reduce_scatter | solution.py:68
  22.8 22.5 %collective-permute-start = (f32[1,2,2,64,192]{4,3,1,2,0:T(8,128)S(1)}, f32[1,2,2,64,192]{4,3,1,2,0:T(8,128)S(1)}, u32[]{:S(2)}, u32[]{:S(2)}) collective-permute-start(f32[1,2,2,64,192]{4,3,1,2,0:T(8,128)S(1)} %pad_maximum_fusion.6), channel_id=1, source_target_pairs={{0,1},{1,2},{2,3},{3,4},{4,5},{5,6},{6,7},{7,8},{8,9},{9,10},{10,1... | collective-permute-start | bytes 589832 | tf_op jit(solution)/shard_map/ppermute | solution.py:51
  23.3 22.3 %collective-permute-start.1 = (f32[1,2,2,64,192]{4,3,1,2,0:T(8,128)S(1)}, f32[1,2,2,64,192]{4,3,1,2,0:T(8,128)S(1)}, u32[]{:S(2)}, u32[]{:S(2)}) collective-permute-start(f32[1,2,2,64,192]{4,3,1,2,0:T(8,128)S(1)} %pad_maximum_fusion.6), channel_id=1, source_target_pairs={{0,15},{1,0},{2,1},{3,2},{4,3},{5,4},{6,5},{7,6},{8,7},{9,8},{10,9... | collective-permute-start | bytes 589832 | tf_op jit(solution)/shard_map/ppermute | solution.py:56
  45.6 8.5 collective-permute-start.2
  45.8 8.5 collective-permute-start.3
  54.3 8.7 collective-permute-start.4
  54.6 8.6 collective-permute-start.5
  63.1 8.7 collective-permute-start.6
  63.4 8.6 collective-permute-start.7
  72.0 8.7 collective-permute-start.8
  72.2 8.6 collective-permute-start.9
  80.8 8.7 collective-permute-start.10
  81.1 8.6 collective-permute-start.11
  89.6 8.5 collective-permute-start.12
  89.9 8.8 collective-permute-start.13
  98.4 8.8 collective-permute-start.14
  255.4 10.0 collective-permute-start.15
  256.1 9.7 collective-permute-start.16
  265.4 9.9 collective-permute-start.17
  265.8 10.0 collective-permute-start.18
  275.3 10.0 collective-permute-start.19
  275.8 10.0 collective-permute-start.20
  285.3 10.0 collective-permute-start.21
  285.9 10.0 collective-permute-start.22
  295.3 10.0 collective-permute-start.23
  295.9 10.0 collective-permute-start.24
  305.3 10.0 collective-permute-start.25
  305.9 11.0 collective-permute-start.26
  315.3 10.0 collective-permute-start.27
  316.9 8.9 collective-permute-start.28
  325.3 9.9 collective-permute-start.29
  481.7 53.5 %collective-permute-start.30 = (f32[1,2,2,64,48]{3,4,2,1,0:T(8,128)S(1)}, f32[1,2,2,64,48]{3,4,2,1,0:T(8,128)S(1)}, u32[]{:S(2)}, u32[]{:S(2)}) collective-permute-start(f32[1,2,2,64,48]{3,4,2,1,0:T(8,128)S(1)} %get-tuple-element.130), channel_id=1, source_target_pairs={{0,1},{1,2},{2,3},{3,4},{4,5},{5,6},{6,7},{7,8},{8,9},{9,10},{10,1... | collective-permute-start | bytes 147464 | tf_op jit(solution)/shard_map/ppermute | solution.py:51
  502.2 33.2 %collective-permute-start.31 = (f32[1,2,2,64,48]{3,4,2,1,0:T(8,128)S(1)}, f32[1,2,2,64,48]{3,4,2,1,0:T(8,128)S(1)}, u32[]{:S(2)}, u32[]{:S(2)}) collective-permute-start(f32[1,2,2,64,48]{3,4,2,1,0:T(8,128)S(1)} %get-tuple-element.130), channel_id=1, source_target_pairs={{0,15},{1,0},{2,1},{3,2},{4,3},{5,4},{6,5},{7,6},{8,7},{9,8},{10,9... | collective-permute-start | bytes 147464 | tf_op jit(solution)/shard_map/ppermute | solution.py:56
  535.2 6.9 collective-permute-start.32
  535.3 6.8 collective-permute-start.33
  542.1 6.8 collective-permute-start.34
  542.1 6.8 collective-permute-start.35
  548.9 6.8 collective-permute-start.36
  548.9 6.8 collective-permute-start.37
  555.7 6.8 collective-permute-start.38
  555.8 6.8 collective-permute-start.39
  562.5 6.8 collective-permute-start.40
  562.6 6.8 collective-permute-start.41
  569.4 6.9 collective-permute-start.43
  576.1 6.9 collective-permute-start.44
  648.4 333.6 %reduce-scatter.8.cloned.1.call-start = ((), (), s32[]{:S(2)}) async-start(), calls=%async_computation.4 | async-start | bytes 4456448 | tf_op jit(solution)/shard_map/reduce_scatter | solution.py:68
  889.1 219.1 %all-reduce.50.cloned.1.call-start = ((), (), s32[]{:S(2)}) async-start(), calls=%async_computation.6 | async-start | bytes 1179648 | tf_op jit(solution)/shard_map/psum | solution.py:242
  1015.2 147.3 %reduce-scatter.10.cloned.1.call-start = ((), (), s32[]{:S(2)}) async-start(), calls=%async_computation.5 | async-start | bytes 208896
  (61 other events, 2540.0 us)
Sparse Core Ops, SparseCore 0:
  648.5 57.0 reduce-scatter.5
  889.2 71.3 reduce-scatter.7
  1015.3 90.5 all-reduce.49
  1109.9 52.5 reduce-scatter.9
